TPU v7x, 32 devices: a whole 2x2x4 slice. The times are simulated.
32 devices in a mesh: grp: 2 (over y), row: 4 (over x, core), ch: 4 (over z).
Axes of the slice: x: 2, y: 2, z: 4, core: 2. Of those that a mesh axis runs over, the one named last changes fastest.
Arguments:
- pair_tensor: bfloat16 [512, 256, 128], P(('grp', 'row'), 'ch'), parts along dimension 0, may hold values from -6 to 6
- cotangent: bfloat16 [512, 256, 128], P(('grp', 'row'), 'ch'), parts along dimension 0, may hold values from -6 to 6
- residue_mask: int32 [512], P('grp'), parts along dimension 0, may hold values 0 or 1
- in_gain: float32 [128], replicated, may hold values from 0.1 to 1.9
- edge_weight: bfloat16 [4, 128, 128], replicated, may hold values from -0.5 to 0.5
- gate_weight: bfloat16 [128, 128], replicated, may hold values from -0.5 to 0.5
- out_gain: float32 [128], replicated, may hold values from 0.1 to 1.9
- out_weight: bfloat16 [128, 128], replicated, may hold values from -0.5 to 0.5
Outputs:
- pair_update: bfloat16 [512, 256, 128], P(('grp', 'row'), 'ch'), parts along dimension 0
- grad_pair: bfloat16 [512, 256, 128], P(('grp', 'row'), 'ch'), parts along dimension 0
There are 2 independent parts, one for each index of `grp`. A program takes and returns all parts, laid end to end along the dimension named above; an argument that names none is the same for every part. Nothing has to cross between parts.
Inputs may be any that keep to these rules, and one draw needn't show every extreme that they name: `residue_mask`: 1 marks a residue that is present, 0 a padded one.
All inputs are finite; a program needn't handle non-finite values.
Results may differ from a plain program's by a relative error of at most 0.0086.
Values may be sent and summed in bfloat16 or wider, within the bound.
A program may use at most 192 MiB of HBM per device.

v0:
```python
import jax
import jax.numpy as jnp
from jax import lax
from jax.sharding import PartitionSpec as P

epsilon = 1e-05


def normalize(values, axis):
    mean_val = jnp.mean(values, axis=axis, keepdims=True)
    centered = values - mean_val
    variance = jnp.mean(centered * centered, axis=axis, keepdims=True)
    inv_scale = lax.rsqrt(variance + epsilon)
    return (centered * inv_scale, inv_scale)


def layer_back(d_hat, hat, inv_scale, axis):
    first = jnp.mean(d_hat, axis=axis, keepdims=True)
    second = jnp.mean(d_hat * hat, axis=axis, keepdims=True)
    return inv_scale * (d_hat - first - hat * second)


def per_device(
    pair_tensor, cotangent, residue_mask, in_gain, edge_weight, gate_weight, out_gain, out_weight
):
    row_count = pair_tensor.shape[0]
    col_count = pair_tensor.shape[1]
    row_start = lax.axis_index("row") * row_count
    col_start = lax.axis_index("ch") * col_count
    live = residue_mask.astype(jnp.float32)
    live_rows = lax.dynamic_slice_in_dim(live, row_start, row_count)
    live_cols = lax.dynamic_slice_in_dim(live, col_start, col_count)
    pair_mask = live_rows[:, None] * live_cols[None, :]
    z_hat, inv_in = normalize(pair_tensor.astype(jnp.float32), -1)
    normed = (z_hat * in_gain).astype(jnp.bfloat16)
    proj = jnp.einsum("rjc,tch->thrj", normed, edge_weight, preferred_element_type=jnp.float32)
    shape_four = proj.shape
    proj_pairs = proj.reshape(2, 2, shape_four[1], row_count, col_count)
    edge_sig = jax.nn.sigmoid(proj_pairs[:, 0])
    edge_val = proj_pairs[:, 1]
    edges = (pair_mask * edge_sig * edge_val).astype(jnp.bfloat16)
    edge_chan = lax.all_to_all(edges, "ch", split_axis=1, concat_axis=3, tiled=True)
    left_c = edge_chan[0]
    right_c = edge_chan[1]
    shard_piece = lax.all_gather(right_c, "row", axis=1, tiled=True)
    block = jnp.einsum("hik,hjk->hij", left_c, shard_piece, preferred_element_type=jnp.float32)
    kept = shard_piece
    tri_full, kept = (block, kept)
    tri = tri_full.astype(jnp.bfloat16)
    tri_home = lax.all_to_all(tri, "ch", split_axis=2, concat_axis=0, tiled=True)
    t_hat, inv_tri = normalize(tri_home.astype(jnp.float32), 0)
    normed_tri = (t_hat * out_gain[:, None, None]).astype(jnp.bfloat16)
    proj_out = jnp.einsum("hrj,hc->rjc", normed_tri, out_weight, preferred_element_type=jnp.float32)
    gate = jax.nn.sigmoid(
        jnp.einsum("rjc,cd->rjd", normed, gate_weight, preferred_element_type=jnp.float32)
    )
    pair_update = (gate * proj_out).astype(jnp.bfloat16)
    grad_in = cotangent.astype(jnp.float32)
    d_out = (grad_in * gate).astype(jnp.bfloat16)
    d_gate = (grad_in * proj_out * gate * (1.0 - gate)).astype(jnp.bfloat16)
    d_ntri = jnp.einsum("rjc,hc->hrj", d_out, out_weight, preferred_element_type=jnp.float32)
    d_tri = layer_back(d_ntri * out_gain[:, None, None], t_hat, inv_tri, 0).astype(jnp.bfloat16)
    d_tri_c = lax.all_to_all(d_tri, "ch", split_axis=0, concat_axis=2, tiled=True)
    d_tri_t = lax.all_to_all(d_tri_c, "row", split_axis=2, concat_axis=1, tiled=True)
    d_left = jnp.einsum("hij,hjk->hik", d_tri_c, kept, preferred_element_type=jnp.float32)
    d_right = jnp.einsum(
        "hij,hik->hjk",
        d_tri_t,
        lax.all_gather(left_c, "row", axis=1, tiled=True),
        preferred_element_type=jnp.float32,
    )
    edge_grads = jnp.stack([d_left, d_right]).astype(jnp.bfloat16)
    grads_home = lax.all_to_all(edge_grads, "ch", split_axis=3, concat_axis=1, tiled=True)
    d_masked = grads_home.astype(jnp.float32) * pair_mask
    d_gates = d_masked * edge_val * edge_sig * (1.0 - edge_sig)
    d_values = d_masked * edge_sig
    d_proj = jnp.stack([d_gates, d_values], axis=1).reshape(shape_four).astype(jnp.bfloat16)
    d_normed = jnp.einsum("thrj,tch->rjc", d_proj, edge_weight, preferred_element_type=jnp.float32)
    d_normed = d_normed + jnp.einsum(
        "rjd,cd->rjc", d_gate, gate_weight, preferred_element_type=jnp.float32
    )
    grad_pair = layer_back(d_normed * in_gain, z_hat, inv_in, -1).astype(jnp.bfloat16)
    return (pair_update, grad_pair)


def solution(mesh):
    in_specs = (
        P(("grp", "row"), "ch", None),
        P(("grp", "row"), "ch", None),
        P("grp"),
        P(),
        P(),
        P(),
        P(),
        P(),
    )
    out_specs = (P(("grp", "row"), "ch", None), P(("grp", "row"), "ch", None))
    return jax.shard_map(
        per_device, mesh=mesh, in_specs=in_specs, out_specs=out_specs, check_vma=False
    )
```

profile of v0, /device:TPU:0, one launch (start us, length us, event | category | flops | bytes accessed | tf_op | source)
XLA Modules:
  0.0 433.1 jit_solution(10194541288206505736)
XLA Ops:
  7.3 0.8 convert_element_type.81
  8.0 1.8 convert_reduce_fusion
  9.9 2.3 fusion.13
  12.3 1.3 fusion.29
  13.6 4.1 fusion.46
  17.6 9.2 %copy.44 = f32[2,1,128,64,64]{4,3,2,0,1:T(8,128)} copy(f32[2,1,128,64,64]{2,4,1,0,3:T(8,128)} %get-tuple-element.8) | data formatting | bytes 8388608
  26.8 9.1 %copy.45 = f32[2,1,128,64,64]{4,3,2,0,1:T(8,128)} copy(f32[2,1,128,64,64]{2,4,1,0,3:T(8,128)} %get-tuple-element.9) | data formatting | bytes 8388608
  36.1 9.0 %copy_bitcast_fusion.1 = bf16[128,2,64,64]{3,2,1,0:T(8,128)(2,1)} fusion(f32[2,1,128,64,64]{4,3,2,0,1:T(8,128)} %copy.45, f32[64,64]{1,0:T(8,128)S(1)} %broadcast_multiply_fusion, f32[2,1,128,64,64]{4,3,2,0,1:T(8,128)} %copy.44), kind=kLoop, calls=%fused_computation.79 | loop fusion | flops 6291456 | bytes 10502144
  45.1 4.9 %reshape.123 = bf16[4,2,131072]{2,1,0:T(2,128)(2,1)S(1)} reshape(bf16[128,2,64,64]{3,2,1,0:T(8,128)(2,1)} %copy_bitcast_fusion.1) | data formatting | bytes 4194304
  50.1 54.6 %all_to_all.69 = bf16[4,2,131072]{2,1,0:T(2,128)(2,1)} all-to-all(bf16[4,2,131072]{2,1,0:T(2,128)(2,1)S(1)} %reshape.123), channel_id=1, replica_groups=mesh['grp'=2,'row'=4,'ch'=4] {'ch'}, dimensions={0} | all-to-all | bytes 4194304 | tf_op jit(solution)/shard_map/all_to_all | solution.py:42
  104.7 5.8 %reshape.124 = bf16[128,2,64,64]{3,2,1,0:T(8,128)(2,1)} reshape(bf16[4,2,131072]{2,1,0:T(2,128)(2,1)} %all_to_all.69) | data formatting | bytes 4194304
  110.5 3.1 copy.29
  113.7 2.3 fusion.47
  116.0 2.0 copy.31
  117.9 2.2 squeeze.12
  120.1 4.9 %copy.30 = bf16[1,32,64,4,64]{4,3,2,1,0:T(4,128)(2,1)} copy(bf16[1,32,64,4,64]{4,2,1,3,0:T(8,128)(2,1)} %get-tuple-element.11) | data formatting | bytes 2097152 | tf_op jit(solution)/shard_map/slice | solution.py:43
  125.0 3.6 squeeze.11
  128.6 25.4 %all-gather.3.cloned.1.call-done = bf16[32,256,256]{2,1,0:T(8,128)(2,1)} async-done(((bf16[32,64,256]{2,1,0:T(8,128)(2,1)}), bf16[32,256,256]{2,1,0:T(8,128)(2,1)}) %all-gather.3.cloned.1.call-update) | async-done | bytes 4194320 | tf_op jit(solution)/shard_map/all_gather | solution.py:45
  154.0 3.6 convolution_convert_fusion.2
  157.5 3.9 copy.32
  161.4 4.4 %reshape.125 = bf16[4,2,65536]{2,1,0:T(2,128)(2,1)} reshape(bf16[256,32,64]{2,1,0:T(8,128)(2,1)} %bitcast.114) | data formatting | bytes 2097152
  165.7 4.6 %all-to-all-start.1 = ((bf16[4,2,65536]{2,1,0:T(2,128)(2,1)}), bf16[4,2,65536]{2,1,0:T(2,128)(2,1)}, u32[]{:S(2)}, u32[]{:S(2)}) async-start(bf16[4,2,65536]{2,1,0:T(2,128)(2,1)} %reshape.125), calls=%async_computation.1 | async-start | bytes 2097152 | tf_op jit(solution)/shard_map/all_to_all | solution.py:50
  170.3 0.2 all-gather.5.cloned.1.call-start
  170.6 0.5 all-gather.5.cloned.1.call-update
  171.1 25.5 %all-to-all-done.1 = bf16[4,2,65536]{2,1,0:T(2,128)(2,1)} async-done(((bf16[4,2,65536]{2,1,0:T(2,128)(2,1)}), bf16[4,2,65536]{2,1,0:T(2,128)(2,1)}, u32[]{:S(2)}, u32[]{:S(2)}) %all-to-all-start.1) | async-done | bytes 1048608 | tf_op jit(solution)/shard_map/all_to_all | solution.py:50
  196.6 3.1 reshape.126
  199.7 3.8 copy.33
  203.5 3.8 copy.34
  207.3 2.7 bitcast_reduce_fusion
  210.0 0.8 copy-done.1
  210.8 0.6 fusion.2
  211.4 0.1 copy-done.11
  211.5 1.5 fusion.25
  213.1 2.9 multiply_convert_fusion.2
  216.0 2.4 bitcast_reduce_fusion.1
  218.4 3.3 fusion.21
  221.7 3.9 copy.35
  225.6 2.7 reshape.127
  228.3 30.0 %all_to_all.70 = bf16[4,2,65536]{2,1,0:T(2,128)(2,1)} all-to-all(bf16[4,2,65536]{2,1,0:T(2,128)(2,1)} %reshape.127), channel_id=1, replica_groups=mesh['grp'=2,'row'=4,'ch'=4] {'ch'}, dimensions={0} | all-to-all | bytes 2097152 | tf_op jit(solution)/shard_map/all_to_all | solution.py:63
  258.3 3.1 reshape.128
  261.4 3.2 copy.36
  264.7 3.5 all_to_all.58
  268.2 3.8 copy.37
  272.0 4.4 %reshape.129 = bf16[4,2,65536]{2,1,0:T(2,128)(2,1)} reshape(bf16[256,32,64]{2,1,0:T(8,128)(2,1)} %bitcast.115) | data formatting | bytes 2097152
  276.3 4.4 %all-to-all-start.3 = ((bf16[4,2,65536]{2,1,0:T(2,128)(2,1)}), bf16[4,2,65536]{2,1,0:T(2,128)(2,1)}, u32[]{:S(2)}, u32[]{:S(2)}) async-start(bf16[4,2,65536]{2,1,0:T(2,128)(2,1)} %reshape.129), calls=%async_computation.3 | async-start | bytes 2097152 | tf_op jit(solution)/shard_map/all_to_all | solution.py:64
  280.8 4.0 fusion.23
  284.8 10.5 %all-to-all-done.3 = bf16[4,2,65536]{2,1,0:T(2,128)(2,1)} async-done(((bf16[4,2,65536]{2,1,0:T(2,128)(2,1)}), bf16[4,2,65536]{2,1,0:T(2,128)(2,1)}, u32[]{:S(2)}, u32[]{:S(2)}) %all-to-all-start.3) | async-done | bytes 1048608 | tf_op jit(solution)/shard_map/all_to_all | solution.py:64
  295.3 3.1 reshape.130
  298.4 2.9 copy.48
  301.3 3.5 all_to_all.62
  304.8 3.1 fusion.24
  308.0 0.2 pad_maximum_fusion.1
  308.2 6.7 %copy.39 = bf16[2,32,64,256]{2,1,0,3:T(8,128)(2,1)} copy(bf16[2,32,64,256]{3,2,1,0:T(8,128)(2,1)S(1)} %pad_maximum_fusion.1) | data formatting | bytes 4194304 | tf_op jit(solution)/shard_map/stack | solution.py:72
  314.8 4.9 %reshape.131 = bf16[4,2,131072]{2,1,0:T(2,128)(2,1)S(1)} reshape(bf16[256,2,32,64]{3,2,1,0:T(8,128)(2,1)} %bitcast.110) | data formatting | bytes 4194304
  319.8 51.7 %all_to_all.71 = bf16[4,2,131072]{2,1,0:T(2,128)(2,1)} all-to-all(bf16[4,2,131072]{2,1,0:T(2,128)(2,1)S(1)} %reshape.131), channel_id=1, replica_groups=mesh['grp'=2,'row'=4,'ch'=4] {'ch'}, dimensions={0} | all-to-all | bytes 4194304 | tf_op jit(solution)/shard_map/all_to_all | solution.py:73
  371.5 5.8 %reshape.132 = bf16[256,2,32,64]{3,2,1,0:T(8,128)(2,1)} reshape(bf16[4,2,131072]{2,1,0:T(2,128)(2,1)} %all_to_all.71) | data formatting | bytes 4194304
  377.3 9.5 %copy.40 = f32[2,32,64,4,64]{4,2,1,3,0:T(8,128)} copy(bf16[2,32,64,4,64]{2,1,0,4,3:T(8,128)(2,1)} %bitcast.108) | data formatting | bytes 6291456 | tf_op jit(solution)/shard_map/convert_element_type | solution.py:74
  386.9 12.5 %multiply_convert_fusion.1 = (bf16[2,1,128,64,64]{4,3,2,0,1:T(8,128)(2,1)S(1)}, bf16[2,1,128,64,64]{4,3,2,0,1:T(8,128)(2,1)}) fusion(f32[2,1,128,64,64]{4,3,2,0,1:T(8,128)} %copy.45, f32[2,1,128,64,64]{4,3,2,0,1:T(8,128)} %bitcast.106, f32[64,64]{1,0:T(8,128)S(1)} %broadcast_multiply_fusion, f32[2,1,128,64,64]{4,3,2,0,1:T(8,128)} %copy.44), kind=kLoop, calls=%fused_computation.5 | loop fusion | flops 11534336 | bytes 16793600 | tf_op jit(solution)/shard_map/convert.8
  399.3 7.3 %pad_maximum_fusion = bf16[2,2,128,64,64]{4,3,2,0,1:T(8,128)(2,1)} fusion(bf16[2,1,128,64,64]{4,3,2,0,1:T(8,128)(2,1)} %get-tuple-element.7, bf16[2,1,128,64,64]{4,3,2,0,1:T(8,128)(2,1)S(1)} %get-tuple-element.6), kind=kLoop, calls=%fused_computation | loop fusion | flops 2097152 | bytes 8388608 | tf_op jit(solution)/shard_map/stack | solution.py:77
  406.7 9.8 %copy.41 = bf16[2,2,128,64,64]{2,4,1,0,3:T(8,128)(2,1)} copy(bf16[2,2,128,64,64]{4,3,2,0,1:T(8,128)(2,1)} %pad_maximum_fusion) | data formatting | bytes 8388608 | tf_op jit(solution)/shard_map/stack | solution.py:77
  416.5 3.6 fusion.37
  420.1 0.1 copy-done.10
  420.2 2.5 fusion.45
  422.7 3.3 fusion.12
  (39 shorter events, 0.3 us)
Async XLA Ops:
  7.2 5.1 %copy-start = (bf16[4,128,128]{2,1,0:T(8,128)(2,1)S(1)}, bf16[4,128,128]{2,1,0:T(8,128)(2,1)}, u32[]{:S(2)}) copy-start(bf16[4,128,128]{2,1,0:T(8,128)(2,1)} %param.12) | copy-start | bytes 393220
  7.2 5.1 %copy-start.2 = (bf16[64,64,128]{2,1,0:T(8,128)(2,1)S(1)}, bf16[64,64,128]{2,1,0:T(8,128)(2,1)}, u32[]{:S(2)}) copy-start(bf16[64,64,128]{2,1,0:T(8,128)(2,1)} %param.8) | copy-start | bytes 3145732
  7.2 5.1 %copy-start.14 = (f32[128]{0:T(128)S(1)}, f32[128]{0:T(128)}, u32[]{:S(2)}) copy-start(f32[128]{0:T(128)} %param.11) | copy-start | bytes 1540
  7.2 146.8 %all-gather.3.cloned.1.call-start = ((), (), s32[]{:S(2)}) async-start(), calls=%async_computation.5 | async-start | bytes 5242880 | tf_op jit(solution)/shard_map/all_gather | solution.py:45
  128.6 28.9 %copy-start.3 = (bf16[32,64,256]{2,1,0:T(8,128)(2,1)}, bf16[32,64,256]{2,1,0:T(8,128)(2,1)S(1)}, u32[]{:S(2)}) copy-start(bf16[32,64,256]{2,1,0:T(8,128)(2,1)S(1)} %squeeze.11) | copy-start | bytes 3145732
  165.7 30.8 %all-to-all-start.1 = ((bf16[4,2,65536]{2,1,0:T(2,128)(2,1)}), bf16[4,2,65536]{2,1,0:T(2,128)(2,1)}, u32[]{:S(2)}, u32[]{:S(2)}) async-start(bf16[4,2,65536]{2,1,0:T(2,128)(2,1)} %reshape.125), calls=%async_computation.1 | async-start | bytes 2097152 | tf_op jit(solution)/shard_map/all_to_all | solution.py:50
  170.3 134.5 %all-gather.5.cloned.1.call-start = ((), (), s32[]{:S(2)}) async-start(), calls=%async_computation.6 | async-start | bytes 5242880 | tf_op jit(solution)/shard_map/all_gather | solution.py:69
  207.3 3.5 copy-start.1
  210.8 0.8 copy-start.11
  210.8 0.8 copy-start.13
  211.5 1.5 copy-start.12
  213.1 2.9 copy-start.4
  213.1 2.9 copy-start.9
  216.0 2.4 copy-start.6
  276.3 18.9 %all-to-all-start.3 = ((bf16[4,2,65536]{2,1,0:T(2,128)(2,1)}), bf16[4,2,65536]{2,1,0:T(2,128)(2,1)}, u32[]{:S(2)}, u32[]{:S(2)}) async-start(bf16[4,2,65536]{2,1,0:T(2,128)(2,1)} %reshape.129), calls=%async_computation.3 | async-start | bytes 2097152 | tf_op jit(solution)/shard_map/all_to_all | solution.py:64
  304.8 3.1 copy-start.8
  416.5 3.6 copy-start.5
  416.5 3.6 copy-start.7
  416.5 3.7 copy-start.10
Sparse Core Ops, SparseCore 0:
  120.2 33.6 all-gather.2
  172.7 34.9 all-gather.4
where the time goes:
time: 441 us; the launch traced here: 433 us
  local copies, waits for them, and re-layouts  142 us (32%)
  blocking collectives  136 us (31%)
  waiting for transfers between devices  61.9 us (14%)
  other arithmetic  43.9 us (10%)
  matrix products  24.8 us (6%)
  between operations  14.6 us (3%)
  starting transfers between devices  9.31 us (2%)
    unnamed x42, local copies, waits for them, and re-layouts  61.6 us
    all_to_all x1, blocking collectives, per_device(): lax.all_to_all(edges, 'ch', split_axis=1, concat_axis=3, tiled=True)  54.6 us
    all_to_all x1, blocking collectives, per_device(): lax.all_to_all(edge_grads, 'ch', split_axis=3, concat_axis=1, tiled=True)  51.7 us
    all_to_all x1, blocking collectives, per_device(): lax.all_to_all(d_tri, 'ch', split_axis=0, concat_axis=2, tiled=True)  30 us
    all_to_all x1, waiting for transfers between devices, per_device(): lax.all_to_all(tri, 'ch', split_axis=2, concat_axis=0, tiled=True)  25.5 us
    all_gather x1, waiting for transfers between devices, per_device(): shard_piece = lax.all_gather(right_c, 'row', axis=1, tiled=True)  25.4 us
    another operation x1, other arithmetic  12.5 us
    all_to_all x3, local copies, waits for them, and re-layouts, per_device(): lax.all_to_all(d_tri, 'ch', split_axis=0, concat_axis=2, tiled=True)  10.5 us
  transfers between devices with their start and end apart: 4, of which 3 were waited for; matrix products, arithmetic and copies ran while one was open for 15% of the time, Pallas kernels for 0%

commit v1 on v0

--- a/solution.py
+++ b/solution.py
@@ -1,6 +1,10 @@
+import functools
+
 import jax
 import jax.numpy as jnp
 from jax import lax
+from jax.experimental import pallas as pl
+from jax.experimental.pallas import tpu as pltpu
 from jax.sharding import PartitionSpec as P
 
 epsilon = 1e-05
@@ -83,6 +87,362 @@
     return (pair_update, grad_pair)
 
 
+GROUP = 4
+TILE = 16
+
+
+def dot(a, b, dims):
+    return lax.dot_general(a, b, ((dims[:1], dims[1:]), ((), ())), preferred_element_type=jnp.float32)
+
+
+def fused_kernel(
+    rows_n, chs_n,
+    x_ref, cot_ref, mask_ref, gin_ref, wt_ref, gw_ref, gout_ref, ow_ref,
+    update_ref, grad_ref,
+    hat_ref, inv_ref, gate_ref, dgate_ref, slope_ref, msig_ref,
+    flip_ref, tri_ref, back_ref, left_ref, right_ref, d_full_ref,
+    send_e, recv_e, send_t, recv_t, send_d, recv_d, send_g, recv_g,
+    send_sem, recv_sem,
+):
+    f32, bf16 = jnp.float32, jnp.bfloat16
+    peers = rows_n * chs_n
+    rows, cols, chans = x_ref.shape
+    half = rows // 2
+    lanes = 2 * cols
+    hidden = ow_ref.shape[0]
+    own_h = hidden // peers
+    part_h = own_h // 2
+    chunks = half // TILE
+    wide = GROUP * lanes
+    groups = TILE // GROUP
+    me = lax.axis_index("row") * chs_n + lax.axis_index("ch")
+
+    def device(flat):
+        return {"row": flat // chs_n, "ch": lax.rem(flat, chs_n)}
+
+    def make_copy(phase, chunk, offset, send, recv, target, slot):
+        return pltpu.make_async_remote_copy(
+            src_ref=send.at[chunk, target],
+            dst_ref=recv.at[chunk, slot],
+            send_sem=send_sem.at[phase, chunk, offset],
+            recv_sem=recv_sem.at[phase, chunk, offset],
+            device_id=device(target),
+            device_id_type=pl.DeviceIdType.MESH,
+        )
+
+    def start_all(phase, chunk, send, recv, fill):
+        def step(offset, carry):
+            target = lax.rem(me + offset, peers)
+            if fill is not None:
+                send[chunk, target] = fill(target)
+            make_copy(phase, chunk, offset, send, recv, target, me).start()
+            return carry
+
+        lax.fori_loop(1, peers, step, 0)
+        if fill is None:
+            recv[chunk, me] = send[chunk, me]
+        else:
+            recv[chunk, me] = fill(me)
+
+    def wait_all(phase, chunk, send, recv, use):
+        if use is not None:
+            use(me)
+
+        def step(offset, carry):
+            target = lax.rem(me + offset, peers)
+            origin = lax.rem(me - offset + peers, peers)
+            make_copy(phase, chunk, offset, send, recv, target, origin).wait_recv()
+            if use is not None:
+                use(origin)
+            return carry
+
+        lax.fori_loop(1, peers, step, 0)
+
+    def wait_sends(phase, chunk, send, recv):
+        def step(offset, carry):
+            target = lax.rem(me + offset, peers)
+            make_copy(phase, chunk, offset, send, recv, target, me).wait_send()
+            return carry
+
+        lax.fori_loop(1, peers, step, 0)
+
+    def pairs_of(ref, first):
+        low = ref[pl.ds(first, GROUP)]
+        high = ref[pl.ds(first + half, GROUP)]
+        return jnp.concatenate([low, high], axis=1).reshape(wide, chans)
+
+    def put_pairs(ref, first, values):
+        values = values.reshape(GROUP, lanes, chans)
+        ref[pl.ds(first, GROUP)] = values[:, :cols]
+        ref[pl.ds(first + half, GROUP)] = values[:, cols:]
+
+    barrier = pltpu.get_barrier_semaphore()
+
+    def greet(offset, carry):
+        pl.semaphore_signal(
+            barrier, inc=1, device_id=device(lax.rem(me + offset, peers)),
+            device_id_type=pl.DeviceIdType.MESH,
+        )
+        return carry
+
+    lax.fori_loop(1, peers, greet, 0)
+
+    for chunk in range(chunks):
+
+        def project(step, carry):
+            first = chunk * TILE + step * GROUP
+            block = chunk * groups + step
+            at = pl.ds(pl.multiple_of(block * wide, wide), wide)
+            x = pairs_of(x_ref, first).astype(f32)
+            centered = x - jnp.mean(x, axis=-1, keepdims=True)
+            inv = lax.rsqrt(jnp.mean(centered * centered, axis=-1, keepdims=True) + epsilon)
+            hat = centered * inv
+            hat_ref[at, :] = hat
+            inv_ref[at, :] = jnp.broadcast_to(inv, (wide, chans))
+            normed = (hat * gin_ref[...]).astype(bf16)
+            gate_ref[at, :] = jax.nn.sigmoid(dot(normed, gw_ref[...], (1, 0)))
+            mask = jnp.concatenate([mask_ref[pl.ds(first + s, 1), :] for s in range(GROUP)], axis=1)
+            for side in range(2):
+                proj = dot(wt_ref[pl.ds(2 * side * hidden, 2 * hidden), :], normed, (1, 1))
+                sig = jax.nn.sigmoid(proj[:hidden])
+                msig = mask * sig
+                edge = msig * proj[hidden:]
+                msig_ref[side, block] = msig
+                slope_ref[side, block] = edge * (1.0 - sig)
+                for s in range(GROUP):
+                    flip_ref[pl.ds(side * hidden * TILE + step * GROUP + s, hidden, stride=TILE), :] = edge[
+                        :, s * lanes : (s + 1) * lanes
+                    ]
+            return carry
+
+        lax.fori_loop(0, groups, project, 0)
+        if chunk == 0:
+            pl.semaphore_wait(barrier, peers - 1)
+
+        def edge_block(owner):
+            size = own_h * TILE
+            return jnp.concatenate(
+                [
+                    flip_ref[pl.ds(pl.multiple_of(side * hidden * TILE + owner * size, size), size), :]
+                    .reshape(own_h, TILE, lanes)
+                    .astype(bf16)
+                    for side in range(2)
+                ],
+                axis=0,
+            )
+
+        start_all(0, chunk, send_e, recv_e, edge_block)
+
+    def assemble(recv, index, out_ref, h):
+        for r in range(rows_n):
+            for chunk in range(chunks):
+                blocks = [recv[chunk, r * chs_n + c, index] for c in range(chs_n)]
+                for ip in range(2):
+                    row = r * rows + ip * half + chunk * TILE
+                    out_ref[h, row : row + TILE, :] = jnp.concatenate(
+                        [b[:, ip * cols : (ip + 1) * cols] for b in blocks], axis=1
+                    )
+
+    def scatter(values, send, chunk, index):
+        for r in range(rows_n):
+            for c in range(chs_n):
+                part = values[r * rows : (r + 1) * rows, c * cols : (c + 1) * cols]
+                send[chunk, r * chs_n + c, index] = jnp.concatenate([part[:half], part[half:]], axis=1)
+
+    for chunk in range(chunks):
+        wait_all(0, chunk, send_e, recv_e, None)
+    for chunk in range(2):
+
+        def multiply(step, carry):
+            h = chunk * part_h + step
+            assemble(recv_e, h, left_ref, h)
+            assemble(recv_e, own_h + h, right_ref, h)
+            tri = dot(left_ref[h], right_ref[h], (1, 1)).astype(bf16)
+            scatter(tri, send_t, chunk, step)
+            return carry
+
+        lax.fori_loop(0, part_h, multiply, 0)
+        start_all(1, chunk, send_t, recv_t, None)
+
+    for chunk in range(2):
+
+        def widen(origin):
+            size = part_h * half
+            row = pl.multiple_of((origin * 2 + chunk) * size, size)
+            tri_ref[pl.ds(row, size), :] = recv_t[chunk, origin].reshape(size, lanes).astype(f32)
+
+        wait_all(1, chunk, send_t, recv_t, widen)
+
+    for chunk in range(chunks):
+
+        def outward(step, carry):
+            first = chunk * TILE + step * GROUP
+            block = chunk * groups + step
+            at = pl.ds(pl.multiple_of(block * wide, wide), wide)
+            tri = jnp.concatenate(
+                [tri_ref[pl.ds(first + s, hidden, stride=half), :] for s in range(GROUP)], axis=1
+            )
+            centered = tri - jnp.mean(tri, axis=0, keepdims=True)
+            inv = lax.rsqrt(jnp.mean(centered * centered, axis=0, keepdims=True) + epsilon)
+            hat = centered * inv
+            gain = gout_ref[...]
+            proj_out = dot((hat * gain).astype(bf16), ow_ref[...], (0, 0))
+            gate = gate_ref[at, :]
+            put_pairs(update_ref, first, (gate * proj_out).astype(bf16))
+            cot_gate = pairs_of(cot_ref, first).astype(f32) * gate
+            dgate_ref[at, :] = (cot_gate * proj_out * (1.0 - gate)).astype(bf16)
+            d_hat = dot(ow_ref[...], cot_gate.astype(bf16), (1, 1)) * gain
+            mean_a = jnp.mean(d_hat, axis=0, keepdims=True)
+            mean_b = jnp.mean(d_hat * hat, axis=0, keepdims=True)
+            d_tri = inv * (d_hat - mean_a - hat * mean_b)
+            for s in range(GROUP):
+                flip_ref[pl.ds(step * GROUP + s, hidden, stride=TILE), :] = d_tri[
+                    :, s * lanes : (s + 1) * lanes
+                ]
+            return carry
+
+        lax.fori_loop(0, groups, outward, 0)
+
+        def d_tri_block(owner):
+            size = own_h * TILE
+            return (
+                flip_ref[pl.ds(pl.multiple_of(owner * size, size), size), :]
+                .reshape(own_h, TILE, lanes)
+                .astype(bf16)
+            )
+
+        start_all(2, chunk, send_d, recv_d, d_tri_block)
+
+    for chunk in range(chunks):
+        wait_all(2, chunk, send_d, recv_d, None)
+    for chunk in range(2):
+
+        def multiply_back(step, carry):
+            h = chunk * part_h + step
+            assemble(recv_d, h, d_full_ref, 0)
+            d_full = d_full_ref[0]
+            scatter(dot(d_full, right_ref[h], (1, 0)).astype(bf16), send_g, chunk, step)
+            scatter(dot(d_full, left_ref[h], (0, 0)).astype(bf16), send_g, chunk, part_h + step)
+            return carry
+
+        lax.fori_loop(0, part_h, multiply_back, 0)
+        start_all(3, chunk, send_g, recv_g, None)
+
+    for chunk in range(2):
+
+        def widen_back(origin):
+            size = part_h * half
+            for side in range(2):
+                row = pl.multiple_of(side * hidden * half + (origin * 2 + chunk) * size, size)
+                back_ref[pl.ds(row, size), :] = (
+                    recv_g[chunk, origin, side * part_h : (side + 1) * part_h].reshape(size, lanes).astype(f32)
+                )
+
+        wait_all(3, chunk, send_g, recv_g, widen_back)
+
+    def inward(block, carry):
+        first = block * GROUP
+        at = pl.ds(pl.multiple_of(block * wide, wide), wide)
+        d_normed = dot(dgate_ref[at, :], gw_ref[...], (1, 1))
+        for side in range(2):
+            d_edge = jnp.concatenate(
+                [
+                    back_ref[pl.ds(side * hidden * half + first + s, hidden, stride=half), :]
+                    for s in range(GROUP)
+                ],
+                axis=1,
+            )
+            d_proj = jnp.concatenate(
+                [
+                    (d_edge * slope_ref[side, block]).astype(bf16),
+                    (d_edge * msig_ref[side, block]).astype(bf16),
+                ],
+                axis=0,
+            )
+            d_normed = d_normed + dot(d_proj, wt_ref[pl.ds(2 * side * hidden, 2 * hidden), :], (0, 0))
+        hat = hat_ref[at, :]
+        d_hat = d_normed * gin_ref[...]
+        mean_a = jnp.mean(d_hat, axis=-1, keepdims=True)
+        mean_b = jnp.mean(d_hat * hat, axis=-1, keepdims=True)
+        grad = inv_ref[at, :] * (d_hat - mean_a - hat * mean_b)
+        put_pairs(grad_ref, first, grad.astype(bf16))
+        return carry
+
+    lax.fori_loop(0, half // GROUP, inward, 0)
+
+    for chunk in range(chunks):
+        wait_sends(0, chunk, send_e, recv_e)
+        wait_sends(2, chunk, send_d, recv_d)
+    for chunk in range(2):
+        wait_sends(1, chunk, send_t, recv_t)
+        wait_sends(3, chunk, send_g, recv_g)
+
+
+def fused_device(
+    rows_n, chs_n,
+    pair_tensor, cotangent, residue_mask, in_gain, edge_weight, gate_weight, out_gain, out_weight,
+):
+    rows, cols, chans = pair_tensor.shape
+    hidden = out_weight.shape[0]
+    peers = rows_n * chs_n
+    own_h = hidden // peers
+    half, lanes, total = rows // 2, 2 * cols, rows * cols
+    chunks = half // TILE
+    side = rows_n * rows
+    blocks = half // GROUP
+    wide = GROUP * lanes
+    live = residue_mask.astype(jnp.float32)
+    live_rows = lax.dynamic_slice_in_dim(live, lax.axis_index("row") * rows, rows)
+    live_cols = lax.dynamic_slice_in_dim(live, lax.axis_index("ch") * cols, cols)
+    mask = live_rows.reshape(2, half).T[:, :, None] * live_cols[None, None, :]
+    f32, bf16 = jnp.float32, jnp.bfloat16
+    vm = pltpu.VMEM
+    scratch = [
+        vm((total, chans), f32),
+        vm((total, chans), f32),
+        vm((total, chans), f32),
+        vm((total, chans), bf16),
+        vm((2, blocks, hidden, wide), f32),
+        vm((2, blocks, hidden, wide), f32),
+        vm((2 * hidden * TILE, lanes), f32),
+        vm((hidden * half, lanes), f32),
+        vm((2 * hidden * half, lanes), f32),
+        vm((own_h, side, side), bf16),
+        vm((own_h, side, side), bf16),
+        vm((1, side, side), bf16),
+    ]
+    for blocks_of in (
+        (chunks, peers, 2 * own_h, TILE, lanes),
+        (2, peers, own_h // 2, half, lanes),
+        (chunks, peers, own_h, TILE, lanes),
+        (2, peers, own_h, half, lanes),
+    ):
+        scratch += [vm(blocks_of, bf16), vm(blocks_of, bf16)]
+    most = max(chunks, 2)
+    scratch += [pltpu.SemaphoreType.DMA((4, most, peers)), pltpu.SemaphoreType.DMA((4, most, peers))]
+    whole = pl.BlockSpec(memory_space=pltpu.VMEM)
+    out = jax.ShapeDtypeStruct((rows, cols, chans), bf16)
+    return pl.pallas_call(
+        functools.partial(fused_kernel, rows_n, chs_n),
+        out_shape=(out, out),
+        in_specs=[whole] * 8,
+        out_specs=(whole, whole),
+        scratch_shapes=scratch,
+        compiler_params=pltpu.CompilerParams(
+            collective_id=0, has_side_effects=True, vmem_limit_bytes=56 * 1024 * 1024
+        ),
+    )(
+        pair_tensor,
+        cotangent,
+        mask.reshape(half, lanes),
+        in_gain.reshape(1, chans),
+        edge_weight.transpose(0, 2, 1).reshape(4 * hidden, chans),
+        gate_weight,
+        out_gain.reshape(hidden, 1),
+        out_weight,
+    )
+
+
 def solution(mesh):
     in_specs = (
         P(("grp", "row"), "ch", None),
@@ -95,6 +455,10 @@
         P(),
     )
     out_specs = (P(("grp", "row"), "ch", None), P(("grp", "row"), "ch", None))
+    rows_n, chs_n = mesh.shape["row"], mesh.shape["ch"]
+    body = per_device
+    if 128 % (rows_n * chs_n) == 0 and (128 // (rows_n * chs_n)) % 2 == 0:
+        body = functools.partial(fused_device, rows_n, chs_n)
     return jax.shard_map(
-        per_device, mesh=mesh, in_specs=in_specs, out_specs=out_specs, check_vma=False
-    )
+        body, mesh=mesh, in_specs=in_specs, out_specs=out_specs, check_vma=False
+    )

time: 441 us -> 172 us (0.39); the launches traced: 433 us -> 172 us
  Pallas kernels: 0 us -> 164 us
  blocking collectives: 136 us -> 0 us
  local copies, waits for them, and re-layouts: 142 us -> 6.07 us
  waiting for transfers between devices: 61.9 us -> 0 us
  other arithmetic: 43.9 us -> 0.61 us
  matrix products: 24.8 us -> 0 us
  between operations: 14.6 us -> 0.68 us
  starting transfers between devices: 9.31 us -> 0 us
    pallas_call x0 -> x1, Pallas kernels: none -> 164 us  [fused_device(): pl.pallas_call(functools.partial(fused_kernel, rows_n, chs_n), out_shape=...]
    all_to_all x3 -> x0, blocking collectives: 136 us -> none  [the longest x1 54.6 us: per_device(): lax.all_to_all(edges, 'ch', split_axis=1, concat_axis=3, tiled=True)]
    unnamed x42 -> x10, local copies, waits for them, and re-layouts: 61.6 us -> 4.05 us
    all_to_all x2 -> x0, waiting for transfers between devices: 36 us -> none  [the longest x1 25.5 us: per_device(): lax.all_to_all(tri, 'ch', split_axis=2, concat_axis=0, tiled=True)]
    all_gather x2 -> x0, waiting for transfers between devices: 25.4 us -> none  [the longest x1 25.4 us: per_device(): shard_piece = lax.all_gather(right_c, 'row', axis=1, tiled=True)]
    convert_element_type x5 -> x0, local copies, waits for them, and re-layouts: 24.9 us -> none  [the longest x1 9.54 us: per_device(): d_masked = grads_home.astype(jnp.float32) * pair_mask]
    dot_general x9 -> x0, matrix products: 24.8 us -> none  [the longest x1 4.01 us: per_device(): jnp.einsum('hij,hjk->hik', d_tri_c, kept, preferred_element_type=jnp.floa...]
    all_to_all x6 -> x0, local copies, waits for them, and re-layouts: 20.1 us -> none  [the longest x3 10.5 us: per_device(): lax.all_to_all(d_tri, 'ch', split_axis=0, concat_axis=2, tiled=True)]
  transfers between devices with their start and end apart: 4 -> 0, of which waited for: 3 -> 0; matrix products, arithmetic and copies ran while one was open for 15% -> 0% of each run, Pallas kernels for 0% -> 0%
where the time goes in v1:
time: 172 us
  Pallas kernels  164 us (95%)
  local copies, waits for them, and re-layouts  6.07 us (4%)
    pallas_call x1, Pallas kernels, fused_device(): pl.pallas_call(functools.partial(fused_kernel, rows_n, chs_n), out_shape=...  164 us
    unnamed x10, local copies, waits for them, and re-layouts  4.05 us

profile of v1, /device:TPU:0, one launch (start us, length us, event | category | flops | bytes accessed | tf_op | source)
XLA Modules:
  0.0 171.6 jit_solution(2308531981688944018)
XLA Ops:
  0.6 0.0 copy-start.2
  0.6 0.0 copy-start.1
  0.7 0.7 copy-done.2
  1.3 0.1 fusion
  1.4 0.1 mul.31
  1.5 0.1 reshape.21
  1.6 0.1 copy.10
  1.7 0.1 mul.27
  1.7 0.1 mul.28
  1.8 0.0 copy-start.3
  1.8 0.6 broadcast_multiply_fusion.mask_ref
  2.4 0.1 copy-done.3
  2.5 0.7 copy.12.gout_ref
  3.2 0.0 copy-done.1
  3.2 0.8 copy.11
  4.0 164.2 %shard_map.95 = (bf16[64,64,128]{2,1,0:T(8,128)(2,1)}, bf16[64,64,128]{2,1,0:T(8,128)(2,1)}) custom-call(bf16[64,64,128]{2,1,0:T(8,128)(2,1)} %x_ref.1, bf16[64,64,128]{2,1,0:T(8,128)(2,1)} %cot_ref.1, f32[32,128]{1,0:T(8,128)} %broadcast_multiply_fusion.mask_ref, f32[1,128]{1,0:T(1,128)} %bitcast.9, bf16[512,128]{1,0:T(8,128)(2,1)} %bitcast.5, ...), custom_call_target="tpu_custom_call" | custom-call | tf_op jit(solution)/shard_map/pallas_call | solution.py:425
  168.2 0.0 copy-start
  168.2 2.4 %copy.15 = bf16[64,64,128]{2,1,0:T(8,128)(2,1)} copy(bf16[64,64,128]{2,1,0:T(8,128)(2,1)} %get-tuple-element.6) | data formatting | bytes 2097152
  170.6 0.0 copy-done
  170.6 1.0 copy.16
  (2 shorter events, 0.0 us)
Async XLA Ops:
  0.6 0.7 copy-start.2
  0.6 2.6 %copy-start.1 = (bf16[4,128,128]{2,1,0:T(8,128)(2,1)S(1)}, bf16[4,128,128]{2,1,0:T(8,128)(2,1)}, u32[]{:S(2)}) copy-start(bf16[4,128,128]{2,1,0:T(8,128)(2,1)} %param.12) | copy-start | bytes 393220
  1.8 0.7 copy-start.3
  168.2 2.4 %copy-start = (bf16[64,64,128]{2,1,0:T(8,128)(2,1)S(1)}, bf16[64,64,128]{2,1,0:T(8,128)(2,1)}, u32[]{:S(2)}) copy-start(bf16[64,64,128]{2,1,0:T(8,128)(2,1)} %get-tuple-element.7) | copy-start | bytes 3145732

commit v2 on v1

v2 whole, which is shorter than its diff:
```python
import functools

import jax
import jax.numpy as jnp
from jax import lax
from jax.experimental import pallas as pl
from jax.experimental.pallas import tpu as pltpu
from jax.sharding import PartitionSpec as P

epsilon = 1e-05


def normalize(values, axis):
    mean_val = jnp.mean(values, axis=axis, keepdims=True)
    centered = values - mean_val
    variance = jnp.mean(centered * centered, axis=axis, keepdims=True)
    inv_scale = lax.rsqrt(variance + epsilon)
    return (centered * inv_scale, inv_scale)


def layer_back(d_hat, hat, inv_scale, axis):
    first = jnp.mean(d_hat, axis=axis, keepdims=True)
    second = jnp.mean(d_hat * hat, axis=axis, keepdims=True)
    return inv_scale * (d_hat - first - hat * second)


def per_device(
    pair_tensor, cotangent, residue_mask, in_gain, edge_weight, gate_weight, out_gain, out_weight
):
    row_count = pair_tensor.shape[0]
    col_count = pair_tensor.shape[1]
    row_start = lax.axis_index("row") * row_count
    col_start = lax.axis_index("ch") * col_count
    live = residue_mask.astype(jnp.float32)
    live_rows = lax.dynamic_slice_in_dim(live, row_start, row_count)
    live_cols = lax.dynamic_slice_in_dim(live, col_start, col_count)
    pair_mask = live_rows[:, None] * live_cols[None, :]
    z_hat, inv_in = normalize(pair_tensor.astype(jnp.float32), -1)
    normed = (z_hat * in_gain).astype(jnp.bfloat16)
    proj = jnp.einsum("rjc,tch->thrj", normed, edge_weight, preferred_element_type=jnp.float32)
    shape_four = proj.shape
    proj_pairs = proj.reshape(2, 2, shape_four[1], row_count, col_count)
    edge_sig = jax.nn.sigmoid(proj_pairs[:, 0])
    edge_val = proj_pairs[:, 1]
    edges = (pair_mask * edge_sig * edge_val).astype(jnp.bfloat16)
    edge_chan = lax.all_to_all(edges, "ch", split_axis=1, concat_axis=3, tiled=True)
    left_c = edge_chan[0]
    right_c = edge_chan[1]
    shard_piece = lax.all_gather(right_c, "row", axis=1, tiled=True)
    block = jnp.einsum("hik,hjk->hij", left_c, shard_piece, preferred_element_type=jnp.float32)
    kept = shard_piece
    tri_full, kept = (block, kept)
    tri = tri_full.astype(jnp.bfloat16)
    tri_home = lax.all_to_all(tri, "ch", split_axis=2, concat_axis=0, tiled=True)
    t_hat, inv_tri = normalize(tri_home.astype(jnp.float32), 0)
    normed_tri = (t_hat * out_gain[:, None, None]).astype(jnp.bfloat16)
    proj_out = jnp.einsum("hrj,hc->rjc", normed_tri, out_weight, preferred_element_type=jnp.float32)
    gate = jax.nn.sigmoid(
        jnp.einsum("rjc,cd->rjd", normed, gate_weight, preferred_element_type=jnp.float32)
    )
    pair_update = (gate * proj_out).astype(jnp.bfloat16)
    grad_in = cotangent.astype(jnp.float32)
    d_out = (grad_in * gate).astype(jnp.bfloat16)
    d_gate = (grad_in * proj_out * gate * (1.0 - gate)).astype(jnp.bfloat16)
    d_ntri = jnp.einsum("rjc,hc->hrj", d_out, out_weight, preferred_element_type=jnp.float32)
    d_tri = layer_back(d_ntri * out_gain[:, None, None], t_hat, inv_tri, 0).astype(jnp.bfloat16)
    d_tri_c = lax.all_to_all(d_tri, "ch", split_axis=0, concat_axis=2, tiled=True)
    d_tri_t = lax.all_to_all(d_tri_c, "row", split_axis=2, concat_axis=1, tiled=True)
    d_left = jnp.einsum("hij,hjk->hik", d_tri_c, kept, preferred_element_type=jnp.float32)
    d_right = jnp.einsum(
        "hij,hik->hjk",
        d_tri_t,
        lax.all_gather(left_c, "row", axis=1, tiled=True),
        preferred_element_type=jnp.float32,
    )
    edge_grads = jnp.stack([d_left, d_right]).astype(jnp.bfloat16)
    grads_home = lax.all_to_all(edge_grads, "ch", split_axis=3, concat_axis=1, tiled=True)
    d_masked = grads_home.astype(jnp.float32) * pair_mask
    d_gates = d_masked * edge_val * edge_sig * (1.0 - edge_sig)
    d_values = d_masked * edge_sig
    d_proj = jnp.stack([d_gates, d_values], axis=1).reshape(shape_four).astype(jnp.bfloat16)
    d_normed = jnp.einsum("thrj,tch->rjc", d_proj, edge_weight, preferred_element_type=jnp.float32)
    d_normed = d_normed + jnp.einsum(
        "rjd,cd->rjc", d_gate, gate_weight, preferred_element_type=jnp.float32
    )
    grad_pair = layer_back(d_normed * in_gain, z_hat, inv_in, -1).astype(jnp.bfloat16)
    return (pair_update, grad_pair)


GROUP = 4
CHUNKS = 4


def dot(a, b, dims):
    return lax.dot_general(a, b, ((dims[:1], dims[1:]), ((), ())), preferred_element_type=jnp.float32)


def fused_kernel(
    rows_n, chs_n,
    x_ref, cot_ref, mask_ref, gin_ref, wt_ref, gw_ref, gout_ref, ow_ref,
    update_ref, grad_ref,
    hat_ref, inv_ref, gate_ref, normed_ref, dgate_ref, slope_ref, msig_ref,
    flip_ref, tri_ref, back_ref, left_ref, right_ref, d_full_ref, own_ref,
    send_e, recv_e, send_p, recv_p, send_t, recv_t, send_d, recv_d, send_g, recv_g,
    send_sem, recv_sem,
):
    f32, bf16 = jnp.float32, jnp.bfloat16
    zs = chs_n // 2
    peers = rows_n * zs
    rows, cols, chans = x_ref.shape
    half = rows // 2
    lanes = 2 * cols
    hidden = ow_ref.shape[0]
    own_h = hidden // peers
    part_h = own_h // CHUNKS
    chunk_h = hidden // CHUNKS
    size = part_h * half
    wide = GROUP * lanes
    groups = half // GROUP
    my_row, my_ch = lax.axis_index("row"), lax.axis_index("ch")
    my_side = my_ch // zs
    me = my_row * zs + lax.rem(my_ch, zs)

    def device(flat, side):
        return {"row": flat // zs, "ch": side * zs + lax.rem(flat, zs)}

    def ahead(offset):
        return lax.rem(me + offset, peers)

    def behind(offset):
        return lax.rem(me - offset + peers, peers)

    def make_copy(phase, chunk, index, source, landing, target, side):
        return pltpu.make_async_remote_copy(
            src_ref=source,
            dst_ref=landing,
            send_sem=send_sem.at[phase, chunk, index],
            recv_sem=recv_sem.at[phase, chunk, index],
            device_id=device(target, side),
            device_id_type=pl.DeviceIdType.MESH,
        )

    def near(phase, chunk, offset, send, recv, slot):
        target = ahead(offset)
        return make_copy(
            phase, chunk, offset, send.at[chunk, target], recv.at[chunk, slot], target, my_side
        )

    def start_near(phase, chunk, send, recv, fill):
        def step(offset, carry):
            if fill is not None:
                send[chunk, ahead(offset)] = fill(ahead(offset))
            near(phase, chunk, offset, send, recv, me).start()
            return carry

        lax.fori_loop(1, peers, step, 0)
        recv[chunk, me] = send[chunk, me] if fill is None else fill(me)

    def wait_near(phase, chunk, send, recv, use):
        if use is not None:
            use(me)

        def step(offset, carry):
            near(phase, chunk, offset, send, recv, behind(offset)).wait_recv()
            if use is not None:
                use(behind(offset))
            return carry

        lax.fori_loop(1, peers, step, 0)

    def across(chunk):
        return make_copy(1, chunk, 0, send_p.at[chunk], recv_p.at[chunk], me, 1 - my_side)

    def spread_near(chunk, offset, slot):
        target = ahead(offset)
        return make_copy(
            3, chunk, offset, send_d.at[chunk, target], recv_d.at[chunk, my_side * peers + slot], target, my_side
        )

    def spread_far(chunk, offset, side, slot):
        target = ahead(offset)
        return make_copy(
            3, chunk, peers + offset, send_d.at[chunk, target], recv_d.at[chunk, side * peers + slot],
            target, 1 - my_side,
        )

    def pairs_of(ref, first):
        low = ref[pl.ds(first, GROUP)]
        high = ref[pl.ds(first + half, GROUP)]
        return jnp.concatenate([low, high], axis=1).reshape(wide, chans)

    def put_pairs(ref, first, values):
        values = values.reshape(GROUP, lanes, chans)
        ref[pl.ds(first, GROUP)] = values[:, :cols]
        ref[pl.ds(first + half, GROUP)] = values[:, cols:]

    def pair_rows(block):
        return pl.ds(pl.multiple_of(block * wide, wide), wide)

    barrier = pltpu.get_barrier_semaphore()

    def greet(offset, carry):
        flat = lax.rem(my_side * peers + me + offset, 2 * peers)
        pl.semaphore_signal(
            barrier, inc=1, device_id=device(lax.rem(flat, peers), flat // peers),
            device_id_type=pl.DeviceIdType.MESH,
        )
        return carry

    lax.fori_loop(1, 2 * peers, greet, 0)

    def prepare(block, carry):
        at = pair_rows(block)
        x = pairs_of(x_ref, block * GROUP).astype(f32)
        centered = x - jnp.mean(x, axis=-1, keepdims=True)
        inv = lax.rsqrt(jnp.mean(centered * centered, axis=-1, keepdims=True) + epsilon)
        hat = centered * inv
        hat_ref[at, :] = hat
        inv_ref[at, :] = jnp.broadcast_to(inv, (wide, chans))
        normed_ref[at, :] = (hat * gin_ref[...]).astype(bf16)
        return carry

    lax.fori_loop(0, groups, prepare, 0)

    for chunk in range(CHUNKS):
        weights = jnp.concatenate(
            [wt_ref[t * hidden + chunk * chunk_h : t * hidden + (chunk + 1) * chunk_h, :] for t in range(4)],
            axis=0,
        )

        def project(block, carry):
            first = block * GROUP
            mask = jnp.concatenate([mask_ref[pl.ds(first + s, 1), :] for s in range(GROUP)], axis=1)
            proj = dot(weights, normed_ref[pair_rows(block), :], (1, 1))
            for side in range(2):
                base = 2 * side * chunk_h
                sig = jax.nn.sigmoid(proj[base : base + chunk_h])
                msig = mask * sig
                edge = msig * proj[base + chunk_h : base + 2 * chunk_h]
                kept = pl.ds(chunk * chunk_h, chunk_h)
                msig_ref[side, block, kept, :] = msig
                slope_ref[side, block, kept, :] = edge * (1.0 - sig)
                for s in range(GROUP):
                    flip_ref[pl.ds(side * chunk_h * half + first + s, chunk_h, stride=half), :] = edge[
                        :, s * lanes : (s + 1) * lanes
                    ]
            return carry

        lax.fori_loop(0, groups, project, 0)
        if chunk == 0:
            pl.semaphore_wait(barrier, 2 * peers - 1)

        def edge_block(owner):
            return jnp.concatenate(
                [
                    flip_ref[pl.ds(pl.multiple_of(side * chunk_h * half + owner * size, size), size), :]
                    .reshape(part_h, half, lanes)
                    .astype(bf16)
                    for side in range(2)
                ],
                axis=0,
            )

        start_near(0, chunk, send_e, recv_e, edge_block)

    def open_gate(block, carry):
        at = pair_rows(block)
        gate_ref[at, :] = jax.nn.sigmoid(dot(normed_ref[at, :], gw_ref[...], (1, 0)))
        return carry

    lax.fori_loop(0, groups, open_gate, 0)

    def assemble(blocks_of, out_ref, h):
        for r in range(rows_n):
            blocks = blocks_of(r)
            for ip in range(2):
                row = r * rows + ip * half
                out_ref[h, row : row + half, :] = jnp.concatenate(
                    [b[:, ip * cols : (ip + 1) * cols] for b in blocks], axis=1
                )

    def scatter(values, send, chunk, index):
        for r in range(rows_n):
            for c in range(zs):
                part = values[r * rows : (r + 1) * rows, c * cols : (c + 1) * cols]
                send[chunk, r * zs + c, index] = jnp.concatenate([part[:half], part[half:]], axis=1)

    reach = zs * cols
    for chunk in range(CHUNKS):
        wait_near(0, chunk, send_e, recv_e, None)

        def multiply(step, carry):
            h = chunk * part_h + step
            for side, out_ref in ((0, left_ref), (1, right_ref)):
                assemble(
                    lambda r: [recv_e[chunk, r * zs + c, side * part_h + step] for c in range(zs)], out_ref, h
                )
            mine = right_ref[h, pl.ds(pl.multiple_of(my_side * reach, reach), reach), :]
            other = right_ref[h, pl.ds(pl.multiple_of((1 - my_side) * reach, reach), reach), :]
            send_p[chunk, step] = dot(left_ref[h], other, (1, 1)).astype(bf16)
            own_ref[h] = dot(left_ref[h], mine, (1, 1))
            return carry

        lax.fori_loop(0, part_h, multiply, 0)
        across(chunk).start()

    for chunk in range(CHUNKS):
        across(chunk).wait_recv()

        def total(step, carry):
            tri = own_ref[chunk * part_h + step] + recv_p[chunk, step].astype(f32)
            scatter(tri.astype(bf16), send_t, chunk, step)
            return carry

        lax.fori_loop(0, part_h, total, 0)
        start_near(2, chunk, send_t, recv_t, None)

    for chunk in range(CHUNKS):

        def widen(origin):
            row = pl.multiple_of((origin * CHUNKS + chunk) * size, size)
            tri_ref[pl.ds(row, size), :] = recv_t[chunk, origin].reshape(size, lanes).astype(f32)

        wait_near(2, chunk, send_t, recv_t, widen)

    def outward(block, carry):
        first = block * GROUP
        at = pair_rows(block)
        tri = jnp.concatenate(
            [tri_ref[pl.ds(first + s, hidden, stride=half), :] for s in range(GROUP)], axis=1
        )
        centered = tri - jnp.mean(tri, axis=0, keepdims=True)
        inv = lax.rsqrt(jnp.mean(centered * centered, axis=0, keepdims=True) + epsilon)
        hat = centered * inv
        gain = gout_ref[...]
        proj_out = dot((hat * gain).astype(bf16), ow_ref[...], (0, 0))
        gate = gate_ref[at, :]
        put_pairs(update_ref, first, (gate * proj_out).astype(bf16))
        cot_gate = pairs_of(cot_ref, first).astype(f32) * gate
        dgate_ref[at, :] = (cot_gate * proj_out * (1.0 - gate)).astype(bf16)
        d_hat = dot(ow_ref[...], cot_gate.astype(bf16), (1, 1)) * gain
        mean_a = jnp.mean(d_hat, axis=0, keepdims=True)
        mean_b = jnp.mean(d_hat * hat, axis=0, keepdims=True)
        d_tri = inv * (d_hat - mean_a - hat * mean_b)
        for s in range(GROUP):
            tri_ref[pl.ds(first + s, hidden, stride=half), :] = d_tri[:, s * lanes : (s + 1) * lanes]
        return carry

    lax.fori_loop(0, groups, outward, 0)

    def d_tri_block(chunk, owner):
        row = pl.multiple_of((owner * CHUNKS + chunk) * size, size)
        return tri_ref[pl.ds(row, size), :].reshape(part_h, half, lanes).astype(bf16)

    for chunk in range(CHUNKS):
        mine = d_tri_block(chunk, me)
        send_d[chunk, me] = mine
        recv_d[chunk, my_side * peers + me] = mine
        spread_far(chunk, 0, my_side, me).start()

        def spread(offset, carry):
            send_d[chunk, ahead(offset)] = d_tri_block(chunk, ahead(offset))
            spread_far(chunk, offset, my_side, me).start()
            spread_near(chunk, offset, me).start()
            return carry

        lax.fori_loop(1, peers, spread, 0)

    for chunk in range(CHUNKS):
        spread_far(chunk, 0, 1 - my_side, me).wait_recv()

        def gathered(offset, carry):
            spread_far(chunk, offset, 1 - my_side, behind(offset)).wait_recv()
            spread_near(chunk, offset, behind(offset)).wait_recv()
            return carry

        lax.fori_loop(1, peers, gathered, 0)

        def multiply_back(step, carry):
            h = chunk * part_h + step
            assemble(
                lambda r: [recv_d[chunk, (c // zs) * peers + r * zs + c % zs, step] for c in range(chs_n)],
                d_full_ref,
                0,
            )
            d_full = d_full_ref[0]
            scatter(dot(d_full, right_ref[h], (1, 0)).astype(bf16), send_g, chunk, step)
            scatter(dot(d_full, left_ref[h], (0, 0)).astype(bf16), send_g, chunk, part_h + step)
            return carry

        lax.fori_loop(0, part_h, multiply_back, 0)
        start_near(4, chunk, send_g, recv_g, None)

    for chunk in range(CHUNKS):

        def widen_back(origin):
            for side in range(2):
                row = pl.multiple_of(((side * CHUNKS + chunk) * peers + origin) * size, size)
                back_ref[pl.ds(row, size), :] = (
                    recv_g[chunk, origin, side * part_h : (side + 1) * part_h].reshape(size, lanes).astype(f32)
                )

        wait_near(4, chunk, send_g, recv_g, widen_back)
    def inward(block, carry):
        first = block * GROUP
        at = pair_rows(block)
        d_normed = dot(dgate_ref[at, :], gw_ref[...], (1, 1))
        for side in range(2):
            d_edge = jnp.concatenate(
                [
                    back_ref[pl.ds(side * hidden * half + first + s, hidden, stride=half), :]
                    for s in range(GROUP)
                ],
                axis=1,
            )
            d_proj = jnp.concatenate(
                [
                    (d_edge * slope_ref[side, block]).astype(bf16),
                    (d_edge * msig_ref[side, block]).astype(bf16),
                ],
                axis=0,
            )
            d_normed = d_normed + dot(d_proj, wt_ref[pl.ds(2 * side * hidden, 2 * hidden), :], (0, 0))
        hat = hat_ref[at, :]
        d_hat = d_normed * gin_ref[...]
        mean_a = jnp.mean(d_hat, axis=-1, keepdims=True)
        mean_b = jnp.mean(d_hat * hat, axis=-1, keepdims=True)
        grad = inv_ref[at, :] * (d_hat - mean_a - hat * mean_b)
        put_pairs(grad_ref, first, grad.astype(bf16))
        return carry

    lax.fori_loop(0, groups, inward, 0)

    for chunk in range(CHUNKS):
        across(chunk).wait_send()
        spread_far(chunk, 0, my_side, me).wait_send()

        def finish(offset, carry):
            near(0, chunk, offset, send_e, recv_e, me).wait_send()
            near(2, chunk, offset, send_t, recv_t, me).wait_send()
            near(4, chunk, offset, send_g, recv_g, me).wait_send()
            spread_near(chunk, offset, me).wait_send()
            spread_far(chunk, offset, my_side, me).wait_send()
            return carry

        lax.fori_loop(1, peers, finish, 0)


def fused_device(
    rows_n, chs_n,
    pair_tensor, cotangent, residue_mask, in_gain, edge_weight, gate_weight, out_gain, out_weight,
):
    rows, cols, chans = pair_tensor.shape
    hidden = out_weight.shape[0]
    peers = rows_n * (chs_n // 2)
    own_h = hidden // peers
    half, lanes, total = rows // 2, 2 * cols, rows * cols
    side = rows_n * rows
    blocks = half // GROUP
    wide = GROUP * lanes
    live = residue_mask.astype(jnp.float32)
    live_rows = lax.dynamic_slice_in_dim(live, lax.axis_index("row") * rows, rows)
    live_cols = lax.dynamic_slice_in_dim(live, lax.axis_index("ch") * cols, cols)
    mask = live_rows.reshape(2, half).T[:, :, None] * live_cols[None, None, :]
    f32, bf16 = jnp.float32, jnp.bfloat16
    vm = pltpu.VMEM
    zs = chs_n // 2
    reach = zs * cols
    part_h = own_h // CHUNKS
    scratch = [
        vm((total, chans), f32),
        vm((total, chans), f32),
        vm((total, chans), f32),
        vm((total, chans), bf16),
        vm((total, chans), bf16),
        vm((2, blocks, hidden, wide), f32),
        vm((2, blocks, hidden, wide), f32),
        vm((2 * (hidden // CHUNKS) * half, lanes), f32),
        vm((hidden * half, lanes), f32),
        vm((2 * hidden * half, lanes), f32),
        vm((own_h, side, reach), bf16),
        vm((own_h, side, reach), bf16),
        vm((1, side, side), bf16),
        vm((own_h, side, reach), f32),
    ]
    edge_slots = vm((CHUNKS, peers, 2 * part_h, half, lanes), bf16)
    part_slots = vm((CHUNKS, part_h, side, reach), bf16)
    tri_slots = vm((CHUNKS, peers, part_h, half, lanes), bf16)
    both_slots = vm((CHUNKS, 2 * peers, part_h, half, lanes), bf16)
    scratch += [edge_slots, edge_slots, part_slots, part_slots, tri_slots, tri_slots]
    scratch += [tri_slots, both_slots, edge_slots, edge_slots]
    sems = pltpu.SemaphoreType.DMA((5, CHUNKS, 2 * peers))
    scratch += [sems, sems]
    whole = pl.BlockSpec(memory_space=pltpu.VMEM)
    out = jax.ShapeDtypeStruct((rows, cols, chans), bf16)
    return pl.pallas_call(
        functools.partial(fused_kernel, rows_n, chs_n),
        out_shape=(out, out),
        in_specs=[whole] * 8,
        out_specs=(whole, whole),
        scratch_shapes=scratch,
        compiler_params=pltpu.CompilerParams(
            collective_id=0, has_side_effects=True, vmem_limit_bytes=56 * 1024 * 1024
        ),
    )(
        pair_tensor,
        cotangent,
        mask.reshape(half, lanes),
        in_gain.reshape(1, chans),
        edge_weight.reshape(4, chans, peers, CHUNKS, part_h)
        .transpose(0, 3, 2, 4, 1)
        .reshape(4 * hidden, chans),
        gate_weight,
        out_gain.reshape(hidden, 1),
        out_weight,
    )


def solution(mesh):
    in_specs = (
        P(("grp", "row"), "ch", None),
        P(("grp", "row"), "ch", None),
        P("grp"),
        P(),
        P(),
        P(),
        P(),
        P(),
    )
    out_specs = (P(("grp", "row"), "ch", None), P(("grp", "row"), "ch", None))
    rows_n, chs_n = mesh.shape["row"], mesh.shape["ch"]
    body = per_device
    owners = rows_n * chs_n // 2
    if chs_n % 2 == 0 and 128 % (owners * CHUNKS) == 0:
        body = functools.partial(fused_device, rows_n, chs_n)
    return jax.shard_map(
        body, mesh=mesh, in_specs=in_specs, out_specs=out_specs, check_vma=False
    )
```

time: 172 us -> 157 us (0.913)
  Pallas kernels: 164 us -> 149 us
    pallas_call x1, Pallas kernels: 164 us -> 149 us  [fused_device(): pl.pallas_call(functools.partial(fused_kernel, rows_n, chs_n), out_shape=...]
    unnamed x10 -> x9, local copies, waits for them, and re-layouts: 4.05 us -> 3.52 us
where the time goes in v2:
time: 157 us; the launch traced here: 156 us
  Pallas kernels  149 us (95%)
  local copies, waits for them, and re-layouts  5.48 us (3%)
    pallas_call x1, Pallas kernels, fused_device(): pl.pallas_call(functools.partial(fused_kernel, rows_n, chs_n), out_shape=...  149 us
    unnamed x9, local copies, waits for them, and re-layouts  3.52 us

profile of v2, /device:TPU:0, one launch (start us, length us, event | category | flops | bytes accessed | tf_op | source)
XLA Modules:
  0.0 156.5 jit_solution(8550434562439263365)
XLA Ops:
  0.6 0.0 copy-start.1
  0.6 0.7 convert_element_type.3
  1.4 0.1 fusion
  1.4 0.1 mul.31
  1.5 0.1 reshape.24
  1.6 0.1 copy.13
  1.7 0.1 mul.27
  1.8 0.1 mul.28
  1.9 0.0 copy-start.2
  1.9 0.6 broadcast_multiply_fusion.mask_ref
  2.5 0.1 copy-done.2
  2.6 0.7 copy.16.gout_ref
  3.3 0.0 copy-done.1
  3.3 0.1 copy.14
  3.4 0.7 copy.15
  4.1 149.0 %shard_map.95 = (bf16[64,64,128]{2,1,0:T(8,128)(2,1)}, bf16[64,64,128]{2,1,0:T(8,128)(2,1)}) custom-call(bf16[64,64,128]{2,1,0:T(8,128)(2,1)} %x_ref.1, bf16[64,64,128]{2,1,0:T(8,128)(2,1)} %cot_ref.1, f32[32,128]{1,0:T(8,128)} %broadcast_multiply_fusion.mask_ref, f32[1,128]{1,0:T(1,128)} %bitcast.11, bf16[512,128]{1,0:T(8,128)(2,1)} %bitcast.8, ...), custom_call_target="tpu_custom_call" | custom-call | tf_op jit(solution)/shard_map/pallas_call | solution.py:496
  153.1 0.0 copy-start
  153.2 2.4 %copy.19 = bf16[64,64,128]{2,1,0:T(8,128)(2,1)} copy(bf16[64,64,128]{2,1,0:T(8,128)(2,1)} %get-tuple-element.6) | data formatting | bytes 2097152
  155.5 0.0 copy-done
  155.5 1.0 copy.20
  (1 shorter events, 0.0 us)
Async XLA Ops:
  0.6 2.7 %copy-start.1 = (bf16[4,128,128]{2,1,0:T(8,128)(2,1)S(1)}, bf16[4,128,128]{2,1,0:T(8,128)(2,1)}, u32[]{:S(2)}) copy-start(bf16[4,128,128]{2,1,0:T(8,128)(2,1)} %param.12) | copy-start | bytes 393220
  1.9 0.7 copy-start.2
  153.1 2.4 %copy-start = (bf16[64,64,128]{2,1,0:T(8,128)(2,1)S(1)}, bf16[64,64,128]{2,1,0:T(8,128)(2,1)}, u32[]{:S(2)}) copy-start(bf16[64,64,128]{2,1,0:T(8,128)(2,1)} %get-tuple-element.7) | copy-start | bytes 3145732

commit v3 on v2

--- a/solution.py
+++ b/solution.py
@@ -99,8 +99,8 @@
     rows_n, chs_n,
     x_ref, cot_ref, mask_ref, gin_ref, wt_ref, gw_ref, gout_ref, ow_ref,
     update_ref, grad_ref,
-    hat_ref, inv_ref, gate_ref, normed_ref, dgate_ref, slope_ref, msig_ref,
-    flip_ref, tri_ref, back_ref, left_ref, right_ref, d_full_ref, own_ref,
+    hat_ref, inv_ref, gate_ref, normed_ref, slope_ref, msig_ref,
+    flip_ref, tri_ref, back_ref, left_ref, right_ref, d_full_ref, own_ref, dhat_ref, ntri_ref,
     send_e, recv_e, send_p, recv_p, send_t, recv_t, send_d, recv_d, send_g, recv_g,
     send_sem, recv_sem,
 ):
@@ -222,11 +222,14 @@
 
     lax.fori_loop(0, groups, prepare, 0)
 
-    for chunk in range(CHUNKS):
-        weights = jnp.concatenate(
+    def chunk_weights(chunk):
+        return jnp.concatenate(
             [wt_ref[t * hidden + chunk * chunk_h : t * hidden + (chunk + 1) * chunk_h, :] for t in range(4)],
             axis=0,
         )
+
+    for chunk in range(CHUNKS):
+        weights = chunk_weights(chunk)
 
         def project(block, carry):
             first = block * GROUP
@@ -265,7 +268,10 @@
 
     def open_gate(block, carry):
         at = pair_rows(block)
-        gate_ref[at, :] = jax.nn.sigmoid(dot(normed_ref[at, :], gw_ref[...], (1, 0)))
+        gate = jax.nn.sigmoid(dot(normed_ref[at, :], gw_ref[...], (1, 0)))
+        gate_ref[at, :] = gate
+        d_out = (pairs_of(cot_ref, block * GROUP).astype(f32) * gate).astype(bf16)
+        dhat_ref[block] = dot(ow_ref[...], d_out, (1, 1)) * gout_ref[...]
         return carry
 
     lax.fori_loop(0, groups, open_gate, 0)
@@ -325,20 +331,14 @@
 
     def outward(block, carry):
         first = block * GROUP
-        at = pair_rows(block)
         tri = jnp.concatenate(
             [tri_ref[pl.ds(first + s, hidden, stride=half), :] for s in range(GROUP)], axis=1
         )
         centered = tri - jnp.mean(tri, axis=0, keepdims=True)
         inv = lax.rsqrt(jnp.mean(centered * centered, axis=0, keepdims=True) + epsilon)
         hat = centered * inv
-        gain = gout_ref[...]
-        proj_out = dot((hat * gain).astype(bf16), ow_ref[...], (0, 0))
-        gate = gate_ref[at, :]
-        put_pairs(update_ref, first, (gate * proj_out).astype(bf16))
-        cot_gate = pairs_of(cot_ref, first).astype(f32) * gate
-        dgate_ref[at, :] = (cot_gate * proj_out * (1.0 - gate)).astype(bf16)
-        d_hat = dot(ow_ref[...], cot_gate.astype(bf16), (1, 1)) * gain
+        ntri_ref[block] = (hat * gout_ref[...]).astype(bf16)
+        d_hat = dhat_ref[block]
         mean_a = jnp.mean(d_hat, axis=0, keepdims=True)
         mean_b = jnp.mean(d_hat * hat, axis=0, keepdims=True)
         d_tri = inv * (d_hat - mean_a - hat * mean_b)
@@ -365,6 +365,18 @@
             return carry
 
         lax.fori_loop(1, peers, spread, 0)
+
+    def update(block, carry):
+        first = block * GROUP
+        at = pair_rows(block)
+        proj_out = dot(ntri_ref[block], ow_ref[...], (0, 0))
+        gate = gate_ref[at, :]
+        put_pairs(update_ref, first, (gate * proj_out).astype(bf16))
+        d_gate = pairs_of(cot_ref, first).astype(f32) * proj_out * gate * (1.0 - gate)
+        gate_ref[at, :] = dot(d_gate.astype(bf16), gw_ref[...], (1, 1))
+        return carry
+
+    lax.fori_loop(0, groups, update, 0)
 
     for chunk in range(CHUNKS):
         spread_far(chunk, 0, 1 - my_side, me).wait_recv()
@@ -401,35 +413,33 @@
                 )
 
         wait_near(4, chunk, send_g, recv_g, widen_back)
-    def inward(block, carry):
-        first = block * GROUP
-        at = pair_rows(block)
-        d_normed = dot(dgate_ref[at, :], gw_ref[...], (1, 1))
-        for side in range(2):
-            d_edge = jnp.concatenate(
-                [
-                    back_ref[pl.ds(side * hidden * half + first + s, hidden, stride=half), :]
-                    for s in range(GROUP)
-                ],
-                axis=1,
-            )
-            d_proj = jnp.concatenate(
-                [
-                    (d_edge * slope_ref[side, block]).astype(bf16),
-                    (d_edge * msig_ref[side, block]).astype(bf16),
-                ],
-                axis=0,
-            )
-            d_normed = d_normed + dot(d_proj, wt_ref[pl.ds(2 * side * hidden, 2 * hidden), :], (0, 0))
-        hat = hat_ref[at, :]
-        d_hat = d_normed * gin_ref[...]
-        mean_a = jnp.mean(d_hat, axis=-1, keepdims=True)
-        mean_b = jnp.mean(d_hat * hat, axis=-1, keepdims=True)
-        grad = inv_ref[at, :] * (d_hat - mean_a - hat * mean_b)
-        put_pairs(grad_ref, first, grad.astype(bf16))
-        return carry
-
-    lax.fori_loop(0, groups, inward, 0)
+        weights = chunk_weights(chunk)
+
+        def inward(block, carry):
+            first = block * GROUP
+            at = pair_rows(block)
+            kept = pl.ds(chunk * chunk_h, chunk_h)
+            parts = []
+            for side in range(2):
+                row = (side * CHUNKS + chunk) * chunk_h * half
+                d_edge = jnp.concatenate(
+                    [back_ref[pl.ds(row + first + s, chunk_h, stride=half), :] for s in range(GROUP)], axis=1
+                )
+                parts.append((d_edge * slope_ref[side, block, kept, :]).astype(bf16))
+                parts.append((d_edge * msig_ref[side, block, kept, :]).astype(bf16))
+            d_normed = gate_ref[at, :] + dot(jnp.concatenate(parts, axis=0), weights, (0, 0))
+            if chunk < CHUNKS - 1:
+                gate_ref[at, :] = d_normed
+                return carry
+            hat = hat_ref[at, :]
+            d_hat = d_normed * gin_ref[...]
+            mean_a = jnp.mean(d_hat, axis=-1, keepdims=True)
+            mean_b = jnp.mean(d_hat * hat, axis=-1, keepdims=True)
+            grad = inv_ref[at, :] * (d_hat - mean_a - hat * mean_b)
+            put_pairs(grad_ref, first, grad.astype(bf16))
+            return carry
+
+        lax.fori_loop(0, groups, inward, 0)
 
     for chunk in range(CHUNKS):
         across(chunk).wait_send()
@@ -472,7 +482,6 @@
         vm((total, chans), f32),
         vm((total, chans), f32),
         vm((total, chans), bf16),
-        vm((total, chans), bf16),
         vm((2, blocks, hidden, wide), f32),
         vm((2, blocks, hidden, wide), f32),
         vm((2 * (hidden // CHUNKS) * half, lanes), f32),
@@ -482,6 +491,8 @@
         vm((own_h, side, reach), bf16),
         vm((1, side, side), bf16),
         vm((own_h, side, reach), f32),
+        vm((blocks, hidden, wide), f32),
+        vm((blocks, hidden, wide), bf16),
     ]
     edge_slots = vm((CHUNKS, peers, 2 * part_h, half, lanes), bf16)
     part_slots = vm((CHUNKS, part_h, side, reach), bf16)

time: 157 us -> 153 us (0.975)
  Pallas kernels: 149 us -> 145 us
    pallas_call x1, Pallas kernels: 149 us -> 145 us  [fused_device(): pl.pallas_call(functools.partial(fused_kernel, rows_n, chs_n), out_shape=...]
where the time goes in v3:
time: 153 us
  Pallas kernels  145 us (95%)
  local copies, waits for them, and re-layouts  5.48 us (4%)
    pallas_call x1, Pallas kernels, fused_device(): pl.pallas_call(functools.partial(fused_kernel, rows_n, chs_n), out_shape=...  145 us
    unnamed x9, local copies, waits for them, and re-layouts  3.52 us

profile of v3, /device:TPU:0, one launch (start us, length us, event | category | flops | bytes accessed | tf_op | source)
XLA Modules:
  0.0 152.8 jit_solution(5182806365607628400)
XLA Ops:
  0.6 0.0 copy-start.1
  0.6 0.7 convert_element_type.3
  1.4 0.1 fusion
  1.4 0.1 mul.31
  1.5 0.1 reshape.24
  1.6 0.1 copy.13
  1.7 0.1 mul.27
  1.8 0.1 mul.28
  1.9 0.0 copy-start.2
  1.9 0.6 broadcast_multiply_fusion.mask_ref
  2.5 0.1 copy-done.2
  2.6 0.7 copy.16.gout_ref
  3.3 0.0 copy-done.1
  3.3 0.1 copy.14
  3.4 0.7 copy.15
  4.1 145.3 %shard_map.95 = (bf16[64,64,128]{2,1,0:T(8,128)(2,1)}, bf16[64,64,128]{2,1,0:T(8,128)(2,1)}) custom-call(bf16[64,64,128]{2,1,0:T(8,128)(2,1)} %x_ref.1, bf16[64,64,128]{2,1,0:T(8,128)(2,1)} %cot_ref.1, f32[32,128]{1,0:T(8,128)} %broadcast_multiply_fusion.mask_ref, f32[1,128]{1,0:T(1,128)} %bitcast.11, bf16[512,128]{1,0:T(8,128)(2,1)} %bitcast.8, ...), custom_call_target="tpu_custom_call" | custom-call | tf_op jit(solution)/shard_map/pallas_call | solution.py:507
  149.5 0.0 copy-start
  149.5 2.4 %copy.19 = bf16[64,64,128]{2,1,0:T(8,128)(2,1)} copy(bf16[64,64,128]{2,1,0:T(8,128)(2,1)} %get-tuple-element.6) | data formatting | bytes 2097152
  151.8 0.0 copy-done
  151.8 1.0 copy.20
  (1 shorter events, 0.0 us)
Async XLA Ops:
  0.6 2.7 %copy-start.1 = (bf16[4,128,128]{2,1,0:T(8,128)(2,1)S(1)}, bf16[4,128,128]{2,1,0:T(8,128)(2,1)}, u32[]{:S(2)}) copy-start(bf16[4,128,128]{2,1,0:T(8,128)(2,1)} %param.12) | copy-start | bytes 393220
  1.9 0.7 copy-start.2
  149.5 2.4 %copy-start = (bf16[64,64,128]{2,1,0:T(8,128)(2,1)S(1)}, bf16[64,64,128]{2,1,0:T(8,128)(2,1)}, u32[]{:S(2)}) copy-start(bf16[64,64,128]{2,1,0:T(8,128)(2,1)} %get-tuple-element.7) | copy-start | bytes 3145732
